TPU v7x, 256 devices: a whole 4x4x8 slice. The times are simulated.
256 devices in a mesh: dp: 8 (over z), fsdp: 32 (over x, y, core).
Axes of the slice: x: 4, y: 4, z: 8, core: 2. Of those that a mesh axis runs over, the one named last changes fastest.
Arguments:
- query_key_value: bfloat16 [131584, 4992], P(('dp', 'fsdp')), may hold values from -6 to 6
- cotangent: bfloat16 [131584, 3200], P(('dp', 'fsdp')), may hold values from -24 to 24
- output_weight: bfloat16 [1664, 3200], P(None, 'fsdp'), may hold values from -0.15625 to 0.15625
- layer_scale: bfloat16 [3200], P('fsdp'), may hold values from 0.25 to 4
- tile_counts: int32 [256], replicated, may hold values from 1 to 2, as said below
Outputs:
- grad_inputs: bfloat16 [131584, 3328], P(('dp', 'fsdp'))
- grad_weight: float32 [1664, 3200], P(None, 'fsdp')
- grad_scale: float32 [3200], P('fsdp')
Inputs may be any that keep to these rules, and one draw needn't show every extreme that they name: `tile_counts`: A device and the device 32 // 2 fsdp places away in the same data group hold at most 3 live tiles together; the live tiles of a device are its first slots.
All inputs are finite; a program needn't handle non-finite values.
Results may differ from a plain program's by a relative error of at most 0.029.
Values may be sent and summed in bfloat16 or wider, within the bound.
A program may use at most 192 MiB of HBM per device.

v0:
```python
import math

import jax
import jax.numpy as jnp
from jax import lax
from jax.sharding import PartitionSpec as P

HEAD_DIM = 128
TILE = 257
SLOTS = 2


def tile_grads(inputs_tile, scaled_tile, weight):
    length = inputs_tile.shape[0]
    head_width = weight.shape[0]
    head_count = head_width // HEAD_DIM
    inverse = 1.0 / math.sqrt(HEAD_DIM)
    queries = inputs_tile[:, :head_width].reshape(length, head_count, HEAD_DIM)
    key_rows = inputs_tile[:, head_width : 2 * head_width].reshape(length, head_count, HEAD_DIM)
    value_rows = inputs_tile[:, 2 * head_width :].reshape(length, head_count, HEAD_DIM)
    scores = (
        jnp.einsum("qhd,khd->hqk", queries, key_rows, preferred_element_type=jnp.float32) * inverse
    )
    probs = jax.nn.softmax(scores, axis=-1).astype(jnp.bfloat16)
    attended = (
        jnp.einsum("hqk,khd->qhd", probs, value_rows, preferred_element_type=jnp.float32)
        .reshape(length, head_width)
        .astype(jnp.bfloat16)
    )
    d_attended = lax.dot_general(
        scaled_tile, weight, (((1,), (1,)), ((), ())), preferred_element_type=jnp.float32
    ).astype(jnp.bfloat16)
    d_heads = d_attended.reshape(length, head_count, HEAD_DIM)
    d_probs = jnp.einsum("qhd,khd->hqk", d_heads, value_rows, preferred_element_type=jnp.float32)
    prob_float = probs.astype(jnp.float32)
    d_scores = (
        prob_float * (d_probs - jnp.sum(d_probs * prob_float, axis=-1, keepdims=True)) * inverse
    ).astype(jnp.bfloat16)
    grad_query = jnp.einsum(
        "hqk,khd->qhd", d_scores, key_rows, preferred_element_type=jnp.float32
    ).reshape(length, head_width)
    grad_key = jnp.einsum(
        "hqk,qhd->khd", d_scores, queries, preferred_element_type=jnp.float32
    ).reshape(length, head_width)
    result = jnp.concatenate([grad_query, grad_key], axis=1).astype(jnp.bfloat16)
    return (result, attended)


def body(query_key_value, cotangent, output_weight, layer_scale, tile_counts):
    n_fsdp = lax.axis_size("fsdp")
    n_groups = lax.axis_size("dp")
    device_id = lax.axis_index("dp") * n_fsdp + lax.axis_index("fsdp")
    own_tiles = tile_counts[device_id]
    weight, gain_full = (
        lax.all_gather(output_weight, "fsdp", axis=1, tiled=True),
        lax.all_gather(layer_scale, "fsdp", axis=0, tiled=True),
    )
    head_width = weight.shape[0]
    width = weight.shape[1]
    work_inputs = query_key_value.reshape(SLOTS, TILE, 3 * head_width)
    work_grads = cotangent.reshape(SLOTS, TILE, width)
    item_count = work_inputs.shape[0]
    scaled_all = (gain_full.astype(jnp.float32) * work_grads.astype(jnp.float32)).astype(
        jnp.bfloat16
    )

    def advance(position, carried):
        grad_buffer, attended_buffer = carried
        slot_index = jnp.where(position < own_tiles, position, item_count - 1)
        inputs_tile = lax.dynamic_index_in_dim(work_inputs, slot_index, 0, keepdims=False)
        scaled_tile = lax.dynamic_index_in_dim(scaled_all, slot_index, 0, keepdims=False)
        grad_inputs, attended = tile_grads(inputs_tile, scaled_tile, weight)
        grad_buffer = lax.dynamic_update_index_in_dim(grad_buffer, grad_inputs, slot_index, 0)
        attended_buffer = lax.dynamic_update_index_in_dim(attended_buffer, attended, slot_index, 0)
        return (grad_buffer, attended_buffer)

    start = (
        jnp.zeros((item_count, TILE, 2 * head_width), jnp.bfloat16),
        jnp.zeros((item_count, TILE, head_width), jnp.bfloat16),
    )
    grad_buffer, attended_buffer = lax.fori_loop(0, own_tiles, advance, start)
    partial_weight = lax.dot_general(
        attended_buffer.reshape(-1, head_width),
        work_grads.reshape(-1, width),
        (((0,), (0,)), ((), ())),
        preferred_element_type=jnp.float32,
    )
    partial_weight = lax.optimization_barrier(partial_weight.astype(jnp.bfloat16)).astype(
        jnp.float32
    )
    shard_weight = lax.psum_scatter(
        partial_weight.astype(jnp.bfloat16), "fsdp", scatter_dimension=1, tiled=True
    )
    summed = lax.psum(shard_weight, "dp").astype(jnp.float32)
    total_rows = query_key_value.shape[0] * n_groups * n_fsdp
    factor = 8.0 / math.sqrt(total_rows)
    grad_weight = factor * layer_scale.astype(jnp.float32)[None, :] * summed
    grad_scale = factor * jnp.sum(output_weight.astype(jnp.float32) * summed, axis=0)
    return (grad_buffer.reshape(SLOTS * TILE, 2 * head_width), grad_weight, grad_scale)


def solution(mesh):
    in_specs = (P(("dp", "fsdp"), None), P(("dp", "fsdp"), None), P(None, "fsdp"), P("fsdp"), P())
    out_specs = (P(("dp", "fsdp"), None), P(None, "fsdp"), P("fsdp"))
    return jax.shard_map(body, mesh=mesh, in_specs=in_specs, out_specs=out_specs, check_vma=False)
```

profile of v0, /device:TPU:2, one launch (start us, length us, event | category | flops | bytes accessed | tf_op | source)
XLA Modules:
  0.0 479.6 jit_solution(17844231021169723700)
XLA Ops:
  7.2 0.7 all-gather.3.cloned.1.call-update
  8.0 1.4 fusion.36
  10.0 0.9 dynamic-update-slice
  10.9 57.3 %all-reduce = bf16[3200]{0:T(1024)(128)(2,1)S(1)} all-reduce(bf16[3200]{0:T(1024)(128)(2,1)S(1)} %dynamic-update-slice), channel_id=1, replica_groups=mesh['dp'=8,'fsdp'=32] {'fsdp'}, use_global_device_ids=true, to_apply=%add | all-reduce | flops 3200 | bytes 12800
  68.2 5.5 %reshape.86 = f32[2,257,3200]{2,1,0:T(8,128)} reshape(bf16[514,3200]{1,0:T(8,128)(2,1)} %param.8) | data formatting | bytes 9868800 | tf_op jit(solution)/shard_map/convert_element_type | solution.py:63
  73.7 5.9 %reshape.83 = bf16[2,257,4992]{2,1,0:T(8,128)(2,1)} reshape(bf16[514,4992]{1,0:T(8,128)(2,1)} %param.7) | data formatting | bytes 10263552 | tf_op jit(solution)/shard_map/reshape | solution.py:60
  79.6 0.6 dynamic_slice.11
  80.2 5.1 %multiply_convert_fusion = bf16[2,257,3200]{2,1,0:T(8,128)(2,1)} fusion(f32[2,257,3200]{2,1,0:T(8,128)} %reshape.86, f32[3200]{0:T(1024)S(1)} %convert_element_type.62), kind=kLoop, calls=%fused_computation.42 | loop fusion | flops 3289600 | bytes 9881600 | tf_op jit(solution)/shard_map/convert_element_type | solution.py:63
  85.2 13.8 %reshape.91 = bf16[3200,1664]{1,0:T(8,128)(2,1)} reshape(bf16[32,100,1664]{2,1,0:T(8,128)(2,1)} %all-gather.3.cloned.1.call-done) | data formatting | bytes 21299200
  99.1 15.9 %copy.41 = bf16[1664,3200]{1,0:T(8,128)(2,1)} copy(bf16[1664,3200]{0,1:T(8,128)(2,1)} %bitcast.38) | data formatting | bytes 21299200 | tf_op jit(solution)/shard_map/while | solution.py:81
  115.0 2.0 broadcast_in_dim.6
  116.9 1.3 broadcast_in_dim.8
  118.3 113.3 %while.12 = (s32[]{:T(128)}, bf16[2,257,3328]{2,1,0:T(8,128)(2,1)}, bf16[2,257,1664]{2,1,0:T(8,128)(2,1)}, s32[]{:T(128)}, bf16[2,257,4992]{2,1,0:T(8,128)(2,1)}...) while((s32[]{:T(128)}, bf16[2,257,3328]{2,1,0:T(8,128)(2,1)}, ...), condition=%wide.region_4.5_spmd, body=%wide.region_0.4_spmd.sunk | while | flops 3858314240 | bytes 95543352 | solution.py:81
  119.8 1.9 dynamic-slice_bitcast_fusion.2
  121.7 1.1 fusion.68
  122.8 0.6 reshape.101
  123.4 2.1 reshape.102
  125.5 1.1 fusion.69
  126.7 3.9 fusion.70
  130.6 0.5 divide_convert_fusion.2
  131.0 1.6 reshape.104
  132.6 7.9 %convolution_convert_fusion.4 = bf16[257,1664]{1,0:T(8,128)(2,1)S(1)} fusion(bf16[1664,3200]{1,0:T(8,128)(2,1)} %get-tuple-element.170, bf16[2,257,3200]{2,1,0:T(8,128)(2,1)} %get-tuple-element.169, s32[]{:T(128)S(6)} %select_n.21), kind=kOutput, calls=%fused_computation.15.clone.1 | convolution fusion | flops 2737374720 | bytes 13194500 | tf_op jit(solution)/shard_map/while/body/dot_general | solution.py:30
  140.6 1.6 reshape.103
  142.2 5.0 %fusion.71 = f32[13,257,257]{1,2,0:T(8,128)} fusion(bf16[257,13,128]{2,1,0:T(8,128)(2,1)} %reshape.103, bf16[257,13,128]{2,1,0:T(8,128)(2,1)} %reshape.104), kind=kOutput, calls=%fused_computation.25.clone.1 | convolution fusion | flops 219811072 | bytes 5145140 | tf_op jit(solution)/shard_map/while/body/qhd,khd->hqk/dot_general | solution.py:34
  147.2 6.6 %fusion.73 = bf16[257,13,128]{2,0,1:T(8,128)(2,1)S(1)} fusion(bf16[13,257,257]{1,2,0:T(8,128)(2,1)S(1)} %divide_convert_fusion.2, f32[13,257,257]{1,2,0:T(8,128)} %fusion.71, bf16[257,13,128]{2,1,0:T(8,128)(2,1)} %copy-done.2), kind=kOutput, calls=%fused_computation.24.clone.1 | convolution fusion | flops 226252768 | bytes 6862414 | tf_op jit(solution)/shard_map/while/body/hqk,khd->qhd/dot_general | solution.py:39
  153.9 1.2 copy.80
  155.1 1.7 concatenate.18
  156.8 7.3 %fusion.72 = bf16[257,13,128]{2,0,1:T(8,128)(2,1)} fusion(bf16[13,257,257]{1,2,0:T(8,128)(2,1)S(1)} %divide_convert_fusion.2, f32[13,257,257]{1,2,0:T(8,128)} %fusion.71, bf16[257,13,128]{2,1,0:T(8,128)(2,1)} %copy-done.1), kind=kOutput, calls=%fused_computation.23.clone.1 | convolution fusion | flops 226252768 | bytes 6862414 | tf_op jit(solution)/shard_map/while/body/hqk,qhd->khd/dot_general | solution.py:42
  164.1 2.3 copy.79
  166.5 2.5 concatenate.17
  168.9 2.6 maximum_dynamic-update-slice_fusion.2
  171.5 1.3 fusion.74
  173.0 0.6 convert_element_type.151
  173.6 1.0 constant_dynamic-update-slice_fusion.2
  175.9 1.9 dynamic-slice_bitcast_fusion.2
  177.8 1.1 fusion.68
  179.0 0.6 reshape.101
  179.6 2.1 reshape.102
  181.7 1.1 fusion.69
  182.8 3.9 fusion.70
  187.2 1.6 reshape.104
  188.8 7.9 %convolution_convert_fusion.4 = bf16[257,1664]{1,0:T(8,128)(2,1)S(1)} fusion(bf16[1664,3200]{1,0:T(8,128)(2,1)} %get-tuple-element.170, bf16[2,257,3200]{2,1,0:T(8,128)(2,1)} %get-tuple-element.169, s32[]{:T(128)S(6)} %select_n.21), kind=kOutput, calls=%fused_computation.15.clone.1 | convolution fusion | flops 2737374720 | bytes 13194500 | tf_op jit(solution)/shard_map/while/body/dot_general | solution.py:30
  196.7 1.6 reshape.103
  198.4 5.0 %fusion.71 = f32[13,257,257]{1,2,0:T(8,128)} fusion(bf16[257,13,128]{2,1,0:T(8,128)(2,1)} %reshape.103, bf16[257,13,128]{2,1,0:T(8,128)(2,1)} %reshape.104), kind=kOutput, calls=%fused_computation.25.clone.1 | convolution fusion | flops 219811072 | bytes 5145140 | tf_op jit(solution)/shard_map/while/body/qhd,khd->hqk/dot_general | solution.py:34
  203.4 6.6 %fusion.73 = bf16[257,13,128]{2,0,1:T(8,128)(2,1)S(1)} fusion(bf16[13,257,257]{1,2,0:T(8,128)(2,1)S(1)} %divide_convert_fusion.2, f32[13,257,257]{1,2,0:T(8,128)} %fusion.71, bf16[257,13,128]{2,1,0:T(8,128)(2,1)} %copy-done.2), kind=kOutput, calls=%fused_computation.24.clone.1 | convolution fusion | flops 226252768 | bytes 6862414 | tf_op jit(solution)/shard_map/while/body/hqk,khd->qhd/dot_general | solution.py:39
  210.0 1.2 copy.80
  211.2 1.7 concatenate.18
  213.0 7.3 %fusion.72 = bf16[257,13,128]{2,0,1:T(8,128)(2,1)} fusion(bf16[13,257,257]{1,2,0:T(8,128)(2,1)S(1)} %divide_convert_fusion.2, f32[13,257,257]{1,2,0:T(8,128)} %fusion.71, bf16[257,13,128]{2,1,0:T(8,128)(2,1)} %copy-done.1), kind=kOutput, calls=%fused_computation.23.clone.1 | convolution fusion | flops 226252768 | bytes 6862414 | tf_op jit(solution)/shard_map/while/body/hqk,qhd->khd/dot_general | solution.py:42
  220.3 2.3 copy.79
  222.6 2.5 concatenate.17
  225.1 2.6 maximum_dynamic-update-slice_fusion.2
  227.7 1.3 fusion.74
  229.1 0.6 convert_element_type.151
  229.7 1.0 constant_dynamic-update-slice_fusion.2
  231.6 1.8 reshape.85
  233.4 13.8 %convolution_convert_fusion.2 = bf16[1664,3200]{1,0:T(8,128)(2,1)} fusion(bf16[514,1664]{1,0:T(8,128)(2,1)S(1)} %reshape.85, bf16[514,3200]{1,0:T(8,128)(2,1)} %param.8), kind=kOutput, calls=%fused_computation.41 | convolution fusion | flops 5479219200 | bytes 15649792 | tf_op jit(solution)/shard_map/dot_general | solution.py:82
  248.2 145.5 %all-reduce.7.cloned.1.call-done = bf16[1664,3200]{1,0:T(8,128)(2,1)} async-done(((bf16[1664,3200]{1,0:T(8,128)(2,1)}), bf16[1664,3200]{1,0:T(8,128)(2,1)}) %all-reduce.7.cloned.1.call-update) | async-done | bytes 10649616
  393.6 2.1 constant_dynamic-slice_fusion
  395.8 2.0 copy.42
  397.8 2.4 reshape.84
  400.2 69.8 %all-reduce.5.cloned.1.call-done = bf16[1664,100]{1,0:T(8,128)(2,1)} async-done(((bf16[1664,100]{1,0:T(8,128)(2,1)}), bf16[1664,100]{1,0:T(8,128)(2,1)}) %all-reduce.5.cloned.1.call-update) | async-done | bytes 332816 | tf_op jit(solution)/shard_map/psum | solution.py:94
  470.0 1.4 fusion.33
  471.4 1.2 copy.43
  472.5 0.5 broadcast_multiply_fusion
  (30 shorter events, 1.0 us)
Async XLA Ops:
  7.2 78.1 %all-gather.3.cloned.1.call-start = ((), (), s32[]{:S(2)}) async-start(), calls=%async_computation.1 | async-start | bytes 11421696 | tf_op jit(solution)/shard_map/all_gather | solution.py:55
  7.9 385.8 %all-reduce.7.cloned.1.call-start = ((), (), s32[]{:S(2)}) async-start(), calls=%async_computation.2 | async-start | bytes 21299200
  73.7 5.9 %copy-start.4 = (s32[256]{0:T(256)S(1)}, s32[256]{0:T(256)}, u32[]{:S(2)}) copy-start(s32[256]{0:T(256)} %param.11) | copy-start | bytes 3076
  123.4 3.2 copy-start.2
  125.5 1.1 copy-start.1
  168.9 2.6 copy-start
  179.6 3.2 copy-start.2
  181.7 1.2 copy-start.1
  225.1 2.6 copy-start
  247.2 150.5 %copy-start.5 = (bf16[100]{0:T(256)(128)(2,1)S(1)}, bf16[100]{0:T(256)(128)(2,1)}, u32[]{:S(2)}) copy-start(bf16[100]{0:T(256)(128)(2,1)} %param.10) | copy-start | bytes 604
  247.2 150.5 %copy-start.3 = (bf16[2,257,3328]{2,1,0:T(8,128)(2,1)S(1)}, bf16[2,257,3328]{2,1,0:T(8,128)(2,1)}, u32[]{:S(2)}) copy-start(bf16[2,257,3328]{2,1,0:T(8,128)(2,1)} %get-tuple-element.42) | copy-start | bytes 10263556
  247.3 222.7 %all-reduce.5.cloned.1.call-start = ((), (), s32[]{:S(2)}) async-start(), calls=%async_computation | async-start | bytes 851968 | tf_op jit(solution)/shard_map/psum | solution.py:94
Sparse Core Ops, SparseCore 0:
  10.6 67.8 all-gather.2
  247.4 146.2 all-reduce.6
  396.7 73.2 all-reduce.4
where the time goes:
time: 481 us; the launch traced here: 480 us
  waiting for transfers between devices  216 us (45%)
  local copies, waits for them, and re-layouts  93.8 us (20%)
  matrix products  72.4 us (15%)
  blocking collectives  57.3 us (12%)
  other arithmetic  20.8 us (4%)
  between operations  15.3 us (3%)
    unnamed x4, waiting for transfers between devices  146 us
    psum x1, waiting for transfers between devices, body(): summed = lax.psum(shard_weight, 'dp').astype(jnp.float32)  69.8 us
    unnamed x1, blocking collectives  57.3 us
    unnamed x13, local copies, waits for them, and re-layouts  21.4 us
    while x1, local copies, waits for them, and re-layouts, body(): grad_buffer, attended_buffer = lax.fori_loop(0, own_tiles, advance, start)  15.9 us
    dot_general x2, matrix products, tile_grads(): lax.dot_general(scaled_tile, weight, (((1,), (1,)), ((), ())), preferred_...  15.8 us
    dot_general x2, matrix products, tile_grads(): jnp.einsum('hqk,qhd->khd', d_scores, queries, preferred_element_type=jnp....  14.7 us
    dot_general x1, matrix products, body(): lax.dot_general(attended_buffer.reshape(-1, head_width), work_grads.resha...  13.8 us
  transfers between devices with their start and end apart: 3, of which 2 were waited for; matrix products, arithmetic and copies ran while one was open for 5% of the time, Pallas kernels for 0%

commit v1 on v0

v1 whole, which is shorter than its diff:
```python
import functools
import math

import jax
import jax.numpy as jnp
from jax import lax
from jax.experimental import pallas as pl
from jax.experimental.pallas import tpu as pltpu
from jax.sharding import PartitionSpec as P

HEAD_DIM = 128
TILE = 257
SLOTS = 2
HEADS = 13
WIDTH = HEADS * HEAD_DIM
MODEL = 3200
SHARD = 100
PADDED = 112
N_FSDP = 32
N_DP = 8
ROWS_DEV = SLOTS * TILE
WINDOW = 258
STARTS = (0, 256)
LANES = ((0, 896), (896, 768))
TOP = 64
BOTTOM = PADDED - TOP
PIECE = 16
MIB = 1024 * 1024
F32 = jnp.float32
BF16 = jnp.bfloat16
MESH = pl.DeviceIdType.MESH


def dot(a, b, dims):
    return lax.dot_general(a, b, (dims, ((), ())), preferred_element_type=F32)


def selection(tile, transposed):
    first = 128 * tile
    owner = first // PADDED
    base = owner * SHARD + jnp.minimum(first - owner * PADDED, SHARD - 1)
    source_tile = jnp.minimum(base // 128, MODEL // 128 - 2)
    shape = (128, 256) if transposed else (256, 128)
    target = lax.broadcasted_iota(jnp.int32, shape, 0 if transposed else 1) + first
    source = lax.broadcasted_iota(jnp.int32, shape, 1 if transposed else 0) + source_tile * 128
    chosen = jnp.zeros(shape, F32)
    for step in range(3):
        index = owner + step
        inside = (target >= index * PADDED) & (target < index * PADDED + SHARD)
        chosen = jnp.where(inside & (source == target - index * (PADDED - SHARD)), 1.0, chosen)
    columns = pl.ds(pl.multiple_of(source_tile * 128, 128), 256)
    return chosen.astype(BF16), columns


def spread_cotangent(cot_ref, padded_ref):
    def one_tile(tile, carry):
        chooser, source = selection(tile, False)
        columns = pl.ds(pl.multiple_of(tile * 128, 128), 128)
        padded_ref[:, columns] = dot(cot_ref[:, source], chooser, ((1,), (0,))).astype(BF16)
        return carry

    lax.fori_loop(0, N_FSDP * PADDED // 128, one_tile, 0)


def head_probs(queries, keys, slot):
    scores = dot(queries, keys, ((1,), (1,)))
    column = lax.broadcasted_iota(jnp.int32, scores.shape, 1)
    row = lax.broadcasted_iota(jnp.int32, scores.shape, 0)
    out_of_tile = WINDOW - 1 if slot == 0 else 0
    scores = jnp.where(column == out_of_tile, -1e30, scores)
    top = jnp.max(scores, axis=1, keepdims=True)
    powers = jnp.exp((scores - top) * (1.0 / math.sqrt(HEAD_DIM)))
    total = jnp.sum(powers, axis=1, keepdims=True)
    probs = powers * (1.0 / total)
    return jnp.where(row == out_of_tile, 0.0, probs).astype(BF16)


def store_window(ref, slot, columns, values):
    if slot == 0:
        ref[0:WINDOW, columns] = values
    else:
        kept = ref[256:272, columns]
        row = lax.broadcasted_iota(jnp.int32, kept.shape, 0)
        ref[256 : 256 + WINDOW, columns] = values
        ref[256:272, columns] = jnp.where(row == 0, kept, values[0:16])


def head_columns(third, head):
    return pl.ds(pl.multiple_of(third * WIDTH + head * HEAD_DIM, 128), HEAD_DIM)


def forward_heads(qkv_ref, live_ref, attended_ref, probs_ref, slots):
    for slot in slots:
        rows = slice(STARTS[slot], STARTS[slot] + WINDOW)

        def one_head(head, carry, slot=slot, rows=rows):
            queries = qkv_ref[rows, head_columns(0, head)]
            keys = qkv_ref[rows, head_columns(1, head)]
            values = qkv_ref[rows, head_columns(2, head)]
            probs = head_probs(queries, keys, slot)
            if probs_ref is not None:
                probs_ref[slot * HEADS + head] = probs
            attended = dot(probs, values, ((1,), (0,)))
            attended = jnp.where(live_ref[slot : slot + 1, :] > 0.5, attended, 0.0).astype(BF16)
            store_window(attended_ref, slot, head_columns(0, head), attended)
            return carry

        lax.fori_loop(0, HEADS, one_head, 0)


def weight_partials(cot_ref, attended_ref, turned_ref, partial_ref):
    tiles = N_FSDP * PADDED // 4 // 128

    def one_line(line, carry):
        def one_tile(tile, inner):
            chooser, source = selection(line * tiles + tile, True)
            rows = pl.ds(pl.multiple_of(tile * 128, 128), 128)
            turned_ref[rows, :] = dot(chooser, cot_ref[:, source], ((1,), (1,))).astype(BF16)
            return inner

        lax.fori_loop(0, tiles, one_tile, 0)
        for start in range(0, WIDTH, 256):
            size = min(256, WIDTH - start)
            columns = slice(start, start + size)
            sums = dot(turned_ref[...], attended_ref[:, columns], ((1,), (0,)))
            partial_ref[line, :, :, :, columns] = sums.astype(BF16).reshape(4, 2, PADDED, size)
        return carry

    lax.fori_loop(0, 4, one_line, 0)


def attended_grads(padded_ref, weight_ref, d_attended_ref, first, last):
    def one_block(columns, size):
        right = weight_ref[:, :, :, :, columns].reshape(N_FSDP * PADDED, size)
        d_attended_ref[:, columns] = dot(padded_ref[...], right, ((1,), (0,))).astype(BF16)

    def one_full(index, carry):
        one_block(pl.ds(pl.multiple_of(index * 256, 256), 256), 256)
        return carry

    lax.fori_loop(first, min(last, WIDTH // 256), one_full, 0)
    if last > WIDTH // 256 and WIDTH % 256:
        one_block(slice(WIDTH // 256 * 256, WIDTH), WIDTH % 256)


def backward_heads(qkv_ref, live_ref, probs_ref, d_attended_ref, grad_ref, slot, first, last):
    inverse = 1.0 / math.sqrt(HEAD_DIM)
    if True:
        rows = slice(STARTS[slot], STARTS[slot] + WINDOW)

        def one_head(head, carry, slot=slot, rows=rows):
            queries = qkv_ref[rows, head_columns(0, head)]
            keys = qkv_ref[rows, head_columns(1, head)]
            values = qkv_ref[rows, head_columns(2, head)]
            if probs_ref is None:
                probs = head_probs(queries, keys, slot).astype(F32)
            else:
                probs = probs_ref[slot * HEADS + head].astype(F32)
            live = live_ref[slot : slot + 1, :] > 0.5
            d_probs = dot(d_attended_ref[rows, head_columns(0, head)], values, ((1,), (1,)))
            weighted = jnp.sum(d_probs * probs, axis=1, keepdims=True)
            d_scores = (probs * ((d_probs - weighted) * inverse)).astype(BF16)
            grad_query = jnp.where(live, dot(d_scores, keys, ((1,), (0,))), 0.0).astype(BF16)
            grad_key = jnp.where(live, dot(d_scores, queries, ((0,), (0,))), 0.0).astype(BF16)
            store_window(grad_ref, slot, head_columns(0, head), grad_query)
            store_window(grad_ref, slot, head_columns(1, head), grad_key)
            return carry

        lax.fori_loop(min(first, HEADS), min(last, HEADS), one_head, 0)


class Copies:
    def __init__(self, send_sems, recv_sems):
        self.send_sems, self.recv_sems, self.count, self.made = send_sems, recv_sems, 0, []

    def start(self, source, target, device):
        copy = pltpu.make_async_remote_copy(
            src_ref=source,
            dst_ref=target,
            send_sem=self.send_sems.at[self.count],
            recv_sem=self.recv_sems.at[self.count],
            device_id=device,
            device_id_type=MESH,
        )
        copy.start()
        self.count += 1
        self.made.append(copy)
        return copy

    def finish(self):
        for copy in self.made:
            copy.wait_send()


class Place:
    def __init__(self):
        self.f = lax.axis_index("fsdp")
        self.z = lax.axis_index("dp")
        self.c = lax.rem(self.f, 2)
        chip = self.f // 2
        self.y = lax.rem(chip, 4)
        self.x = chip // 4

    def device(self, x, y, c):
        return (self.z, ((x * 4) + y) * 2 + c)

    def around(self, axis, steps):
        u = lax.rem((self.x if axis == 0 else self.y) + 4 + steps, 4)
        return u

    def neighbour(self, axis, steps):
        u = self.around(axis, steps)
        return self.device(u, self.y, self.c) if axis == 0 else self.device(self.x, u, self.c)

    def sibling(self):
        return self.device(self.x, self.y, 1 - self.c)

    def layer(self, steps):
        return lax.rem(self.z + steps, N_DP)

    def greet(self):
        barrier = pltpu.get_barrier_semaphore()
        others = [self.sibling()]
        for axis in (0, 1):
            for step in (1, -1):
                others.append(self.neighbour(axis, step))
        for step in range(1, N_DP):
            others.append((self.layer(step), self.f))
        for other in others:
            pl.semaphore_signal(barrier, inc=1, device_id=other, device_id_type=MESH)
        pl.semaphore_wait(barrier, len(others))


def pick(first, u, v):
    return (u, v) if first == 0 else (v, u)


class WeightGather:
    def __init__(self, place, copies, weight_ref):
        self.place, self.copies, self.weight = place, copies, weight_ref
        self.own = (place.x, place.y)

    def block(self, half, x, y, rows=slice(0, PADDED)):
        start, size = LANES[half]
        return self.weight.at[x, y, self.place.c, rows, slice(start, start + size)]

    def send(self, half, axis, step, x, y, rows=slice(0, PADDED)):
        ref = self.block(half, x, y, rows)
        return self.copies.start(ref, ref, self.place.neighbour(axis, step))

    def begin(self):
        self.first = {}
        self.second = {}
        for half in (0, 1):
            for step in (1, -1):
                self.first[half, step] = self.send(half, half, step, *self.own)
        for half in (0, 1):
            self.send_second(half, 0)

    def send_second(self, half, away):
        u, v = self.place.around(half, away), self.place.around(1 - half, 0)
        for step in (1, -1):
            self.second[half, away, step] = self.send(half, 1 - half, step, *pick(half, u, v))

    def middle(self):
        self.far = {}
        place = self.place
        for step in (1, -1):
            for half in (0, 1):
                self.first[half, step].wait_recv()
                u, v = place.around(half, -step), place.around(1 - half, 0)
                part = slice(0, TOP) if step == 1 else slice(TOP, PADDED)
                self.far[half, step] = self.send(half, half, step, *pick(half, u, v), part)
                self.send_second(half, -step)
        for half in (0, 1):
            for step in (1, -1):
                self.far[half, step].wait_recv()
            self.send_second(half, 2)

    def spread(self):
        place = self.place
        self.last = {}
        for away in (0, -1, 1, 2):
            for half in (0, 1):
                for step in (1, -1):
                    self.second[half, away, step].wait_recv()
                    u, v = place.around(half, away), place.around(1 - half, -step)
                    part = slice(0, TOP) if step == 1 else slice(TOP, PADDED)
                    self.last[half, away, step] = self.send(
                        half, 1 - half, step, *pick(half, u, v), part
                    )

    def share(self):
        place = self.place
        self.shared = []
        for away in (0, -1, 1, 2):
            for half in (0, 1):
                for step in (1, -1):
                    self.last[half, away, step].wait_recv()
                u = place.around(half, away)
                start, size = LANES[half]
                line = (u, slice(None)) if half == 0 else (slice(None), u)
                ref = self.weight.at[*line, place.c, :, slice(start, start + size)]
                self.shared.append(self.copies.start(ref, ref, place.sibling()))

    def end(self):
        for copy in self.shared:
            copy.wait_recv()


class GradReduce:
    def __init__(self, place, copies, partial_ref, sums_ref, buffers, layers_ref, result_ref):
        self.place, self.copies = place, copies
        self.partial, self.sums, self.buffers = partial_ref, sums_ref, buffers
        self.layers, self.result = layers_ref, result_ref

    def line(self, half, away):
        u = self.place.around(half, away)
        return (u, slice(None)) if half == 0 else (slice(None), u)

    def lanes(self, half):
        return slice(LANES[half][0], LANES[half][0] + LANES[half][1])

    def begin(self):
        self.crossed = {}
        for away in (2, 1, -1, 0):
            for half in (0, 1):
                line, lanes = self.line(half, away), self.lanes(half)
                self.crossed[half, away] = self.copies.start(
                    self.partial.at[*line, 1 - self.place.c, :, lanes],
                    self.sums.at[*line, :, lanes],
                    self.place.sibling(),
                )

    def chunk(self, half, away, v):
        u = self.place.around(half, away)
        return pick(half, u, v)

    def add_own(self, half, away):
        self.crossed[half, away].wait_recv()
        lanes = self.lanes(half)

        def one(v, carry):
            x, y = self.chunk(half, away, v)
            total = self.sums[x, y, :, lanes].astype(F32)
            total += self.partial[x, y, self.place.c, :, lanes].astype(F32)
            self.sums[x, y, :, lanes] = total.astype(BF16)
            return carry

        lax.fori_loop(0, 4, one, 0)

    def group(self, half, away, first):
        u = self.place.around(half, away)
        part = slice(first, first + 2)
        return self.sums.at[*pick(half, u, part), :, self.lanes(half)]

    def first_sends(self):
        self.near, self.far = {}, {}
        place = self.place
        for half in (0, 1):
            self.add_own(half, 2)
            for step in (1, -1):
                self.far[half, step] = self.copies.start(
                    self.group(half, 2, 0 if step == 1 else 2),
                    self.buffers[half][0].at[0 if step == 1 else 1],
                    place.neighbour(half, step),
                )
        for step in (1, -1):
            for half in (0, 1):
                self.add_own(half, step)
                other = 2 if step == 1 else 0
                self.near[half, step, 0] = self.copies.start(
                    self.group(half, step, other),
                    self.buffers[half][1].at[0 if step == 1 else 1, slice(other, other + 2)],
                    place.neighbour(half, step),
                )
        for half in (0, 1):
            self.add_own(half, 0)

    def first_forward(self):
        place = self.place
        for step in (1, -1):
            for half in (0, 1):
                side, start = (0, 0) if step == 1 else (1, 2)
                self.far[half, step].wait_recv()
                lanes = self.lanes(half)
                arrived = self.buffers[half][0]

                def one(v, carry, half=half, side=side, start=start, lanes=lanes, arrived=arrived):
                    x, y = self.chunk(half, step, start + v)
                    total = self.sums[x, y, :, lanes].astype(F32)
                    total += arrived[side, v].astype(F32)
                    self.sums[x, y, :, lanes] = total.astype(BF16)
                    return carry

                lax.fori_loop(0, 2, one, 0)
                self.near[half, step, 1] = self.copies.start(
                    self.group(half, step, start),
                    self.buffers[half][1].at[side, slice(start, start + 2)],
                    place.neighbour(half, step),
                )

    def first_end(self):
        for half in (0, 1):
            for step in (1, -1):
                self.near[half, step, 0].wait_recv()
                self.near[half, step, 1].wait_recv()
            lanes = self.lanes(half)
            arrived = self.buffers[half][1]

            def one(v, carry, half=half, lanes=lanes, arrived=arrived):
                x, y = self.chunk(half, 0, v)
                total = self.sums[x, y, :, lanes].astype(F32)
                total += arrived[0, v].astype(F32) + arrived[1, v].astype(F32)
                self.sums[x, y, :, lanes] = total.astype(BF16)
                return carry

            lax.fori_loop(0, 4, one, 0)
            self.second_sends(half)

    def mine(self, half, away):
        place = self.place
        return pick(half, place.around(half, 0), place.around(1 - half, away))

    def second_sends(self, half):
        place, lanes = self.place, self.lanes(half)
        if half == 0:
            self.far2, self.near2 = {}, {}
        for step in (1, -1):
            side = 0 if step == 1 else 1
            rows = slice(0, TOP) if step == 1 else slice(TOP, PADDED)
            self.far2[half, step] = self.copies.start(
                self.sums.at[*self.mine(half, 2), rows, lanes],
                self.buffers[half][2].at[side, rows],
                place.neighbour(1 - half, step),
            )
        for step in (1, -1):
            side = 0 if step == 1 else 1
            rows = slice(TOP, PADDED) if step == 1 else slice(0, TOP)
            self.near2[half, step, 0] = self.copies.start(
                self.sums.at[*self.mine(half, step), rows, lanes],
                self.buffers[half][3].at[side, rows],
                place.neighbour(1 - half, step),
            )

    def second_forward(self):
        place = self.place
        for half in (0, 1):
            lanes = self.lanes(half)
            for step in (1, -1):
                side = 0 if step == 1 else 1
                rows = slice(0, TOP) if step == 1 else slice(TOP, PADDED)
                self.far2[half, step].wait_recv()
                x, y = self.mine(half, step)
                total = self.sums[x, y, rows, lanes].astype(F32)
                total += self.buffers[half][2][side, rows].astype(F32)
                self.sums[x, y, rows, lanes] = total.astype(BF16)
                self.near2[half, step, 1] = self.copies.start(
                    self.sums.at[x, y, rows, lanes],
                    self.buffers[half][3].at[side, rows],
                    place.neighbour(1 - half, step),
                )

    def second_end(self):
        layers = self.layers
        layers[0, PADDED:128, :] = jnp.zeros((128 - PADDED, WIDTH), BF16)
        for half in (0, 1):
            lanes = self.lanes(half)
            for step in (1, -1):
                self.near2[half, step, 0].wait_recv()
                self.near2[half, step, 1].wait_recv()
            x, y = self.mine(half, 0)
            arrived = self.buffers[half][3]
            total = self.sums[x, y, :, lanes].astype(F32)
            total += arrived[0].astype(F32) + arrived[1].astype(F32)
            layers[0, 0:PADDED, lanes] = total.astype(BF16)

    def piece(self, z):
        return pl.ds(pl.multiple_of(z * PIECE, PIECE), PIECE)

    def layer_sends(self):
        place = self.place
        self.up = [
            self.copies.start(
                self.layers.at[0, self.piece(place.layer(step))],
                self.layers.at[1, slice(step * PIECE, step * PIECE + PIECE)],
                (place.layer(step), place.f),
            )
            for step in range(1, N_DP)
        ]

    def layer_sums(self):
        place = self.place
        own = self.piece(place.z)
        total = self.layers[0, own, :].astype(F32)
        for step in range(1, N_DP):
            self.up[step - 1].wait_recv()
            total += self.layers[1, step * PIECE : step * PIECE + PIECE, :].astype(F32)
        self.result[own, :] = total.astype(BF16)
        self.down = [
            self.copies.start(
                self.result.at[own], self.result.at[own], (place.layer(step), place.f)
            )
            for step in range(1, N_DP)
        ]

    def end(self):
        for copy in self.down:
            copy.wait_recv()


N_COPIES = 48 + 8 + 12 + 12 + 14


def whole_kernel(
    shard_ref, qkv_ref, cot_ref, live_ref, grad_ref, result_ref, weight_ref, partial_ref, sums_ref,
    b00, b01, b02, b03, b10, b11, b12, b13, layers_ref, padded_ref, turned_ref, attended_ref,
    probs_ref, send_sems, recv_sems,
):
    place = Place()
    copies = Copies(send_sems, recv_sems)
    weight_ref[place.x, place.y, place.c] = shard_ref[...]
    place.greet()
    gather = WeightGather(place, copies, weight_ref)
    reduce = GradReduce(
        place, copies, partial_ref, sums_ref, ((b00, b01, b02, b03), (b10, b11, b12, b13)),
        layers_ref, result_ref,
    )

    def backward(slot, first, last):
        backward_heads(
            qkv_ref, live_ref, probs_ref, attended_ref, grad_ref, slot, first, last
        )

    gather.begin()
    forward_heads(qkv_ref, live_ref, attended_ref, probs_ref, (0,))
    gather.middle()
    forward_heads(qkv_ref, live_ref, attended_ref, probs_ref, (1,))
    gather.spread()
    weight_partials(cot_ref, attended_ref, turned_ref, partial_ref)
    reduce.begin()
    gather.share()
    spread_cotangent(cot_ref, padded_ref)
    gather.end()
    reduce.first_sends()
    attended_grads(padded_ref, weight_ref, attended_ref, 0, 7)
    reduce.first_forward()
    backward(0, 0, 7)
    reduce.first_end()
    backward(0, 7, 10)
    reduce.second_forward()
    backward(0, 10, HEADS)
    reduce.second_end()
    reduce.layer_sends()
    backward(1, 0, 6)
    reduce.layer_sums()
    backward(1, 6, HEADS)
    reduce.end()
    copies.finish()


def exchange_buffers():
    shapes = []
    for _, size in LANES:
        shapes += [
            pltpu.VMEM((2, 2, PADDED, size), BF16),
            pltpu.VMEM((2, 4, PADDED, size), BF16),
            pltpu.VMEM((2, PADDED, size), BF16),
            pltpu.VMEM((2, PADDED, size), BF16),
        ]
    return shapes


VMEM = pl.BlockSpec(memory_space=pltpu.VMEM)


def whole(shard, qkv, cot, live):
    return pl.pallas_call(
        whole_kernel,
        out_shape=(
            jax.ShapeDtypeStruct((ROWS_DEV, 2 * WIDTH), BF16),
            jax.ShapeDtypeStruct((128, WIDTH), BF16),
        ),
        in_specs=[VMEM] * 4,
        out_specs=[VMEM] * 2,
        scratch_shapes=[
            pltpu.VMEM((4, 4, 2, PADDED, WIDTH), BF16),
            pltpu.VMEM((4, 4, 2, PADDED, WIDTH), BF16),
            pltpu.VMEM((4, 4, PADDED, WIDTH), BF16),
        ]
        + exchange_buffers()
        + [
            pltpu.VMEM((2, 128, WIDTH), BF16),
            pltpu.VMEM((ROWS_DEV, N_FSDP * PADDED), BF16),
            pltpu.VMEM((N_FSDP * PADDED // 4, ROWS_DEV), BF16),
            pltpu.VMEM((ROWS_DEV, WIDTH), BF16),
            pltpu.VMEM((SLOTS * HEADS, WINDOW, WINDOW), BF16),
            pltpu.SemaphoreType.DMA((N_COPIES,)),
            pltpu.SemaphoreType.DMA((N_COPIES,)),
        ],
        compiler_params=pltpu.CompilerParams(
            collective_id=0, has_side_effects=True, vmem_limit_bytes=62 * MIB
        ),
        name="whole",
    )(shard, qkv, cot, live)


def body(query_key_value, cotangent, output_weight, layer_scale, tile_counts):
    device_id = lax.axis_index("dp") * N_FSDP + lax.axis_index("fsdp")
    own_tiles = tile_counts[device_id]
    live = (jnp.arange(8)[:, None] < own_tiles).astype(F32) * jnp.ones((1, 128), F32)
    scale = layer_scale.astype(F32)[None, :]
    scaled = (output_weight.astype(F32) * scale).astype(BF16)
    shard = jnp.pad(scaled.T, ((0, PADDED - SHARD), (0, 0)))

    grads, summed = whole(shard, query_key_value, cotangent, live)
    summed = summed[:SHARD].T.astype(F32)
    factor = 8.0 / math.sqrt(ROWS_DEV * N_FSDP * N_DP)
    grad_weight = factor * scale * summed
    grad_scale = factor * jnp.sum(output_weight.astype(F32) * summed, axis=0)
    return (grads, grad_weight, grad_scale)


def solution(mesh):
    in_specs = (P(("dp", "fsdp"), None), P(("dp", "fsdp"), None), P(None, "fsdp"), P("fsdp"), P())
    out_specs = (P(("dp", "fsdp"), None), P(None, "fsdp"), P("fsdp"))
    return jax.shard_map(body, mesh=mesh, in_specs=in_specs, out_specs=out_specs, check_vma=False)
```

time: 481 us -> 154 us (0.32)
  waiting for transfers between devices: 216 us -> 0 us
  Pallas kernels: 0 us -> 138 us
  local copies, waits for them, and re-layouts: 93.8 us -> 6.67 us
  matrix products: 72.4 us -> 0 us
  blocking collectives: 57.3 us -> 0 us
  other arithmetic: 20.8 us -> 5.01 us
  between operations: 15.3 us -> 0.68 us
    unnamed x4 -> x0, waiting for transfers between devices: 146 us -> none
    pallas_call x0 -> x1, Pallas kernels: none -> 138 us  [whole(): pl.pallas_call(whole_kernel, out_shape=(jax.ShapeDtypeStruct((ROWS_DEV, 2...]
    dot_general x13 -> x0, matrix products: 72.4 us -> none  [the longest x2 15.8 us: tile_grads(): lax.dot_general(scaled_tile, weight, (((1,), (1,)), ((), ())), preferred_...]
    psum x1 -> x0, waiting for transfers between devices: 69.8 us -> none  [body(): summed = lax.psum(shard_weight, 'dp').astype(jnp.float32)]
    unnamed x1 -> x0, blocking collectives: 57.3 us -> none
    reshape x11 -> x0, local copies, waits for them, and re-layouts: 22 us -> none  [the longest x1 5.85 us: body(): work_inputs = query_key_value.reshape(SLOTS, TILE, 3 * head_width)]
    unnamed x13 -> x5, local copies, waits for them, and re-layouts: 21.4 us -> 3.98 us
    while x13 -> x0, local copies, waits for them, and re-layouts: 15.9 us -> none  [the longest x1 15.9 us: body(): grad_buffer, attended_buffer = lax.fori_loop(0, own_tiles, advance, start)]
  transfers between devices with their start and end apart: 3 -> 0, of which waited for: 2 -> 0; matrix products, arithmetic and copies ran while one was open for 5% -> 0% of each run, Pallas kernels for 0% -> 0%
where the time goes in v1:
time: 154 us; the launch traced here: 151 us
  Pallas kernels  138 us (90%)
  local copies, waits for them, and re-layouts  6.67 us (4%)
  other arithmetic  5.01 us (3%)
    pallas_call x1, Pallas kernels, whole(): pl.pallas_call(whole_kernel, out_shape=(jax.ShapeDtypeStruct((ROWS_DEV, 2...  138 us
    unnamed x5, local copies, waits for them, and re-layouts  3.98 us

profile of v1, /device:TPU:2, one launch (start us, length us, event | category | flops | bytes accessed | tf_op | source)
XLA Modules:
  0.0 150.6 jit_solution(9624449792564499976)
XLA Ops:
  0.6 0.7 convert_element_type.27
  1.3 1.1 fusion.2
  2.4 0.8 pad.4.shard_ref
  3.2 1.3 dynamic_slice.3
  4.4 0.6 compare_convert_fusion
  5.1 0.7 mul.41.live_ref
  5.7 0.0 copy-start.1
  5.7 0.0 copy-start
  5.7 138.2 %whole.1 = (bf16[514,3328]{1,0:T(8,128)(2,1)}, bf16[128,1664]{1,0:T(8,128)(2,1)}) custom-call(bf16[112,1664]{1,0:T(8,128)(2,1)} %pad.4.shard_ref, bf16[514,4992]{1,0:T(8,128)(2,1)} %qkv_ref.1, bf16[514,3200]{1,0:T(8,128)(2,1)} %cot_ref.1, f32[8,128]{1,0:T(8,128)} %mul.41.live_ref), custom_call_target="tpu_custom_call" | custom-call | tf_op jit(solution)/shard_map/whole/pallas_call | solution.py:578
  144.0 0.0 copy-done.1
  144.0 0.0 copy-done
  144.0 2.1 %fusion.1 = (f32[100]{0:T(128)S(1)}, f32[1664,100]{0,1:T(8,128)}) fusion(bf16[1664,100]{0,1:T(8,128)(2,1)S(1)} %copy-done, bf16[128,1664]{1,0:T(8,128)(2,1)} %get-tuple-element.6, f32[100]{0:T(128)S(1)} %broadcast_multiply_fusion.1), kind=kLoop, calls=%fused_computation.3 | loop fusion | flops 831900 | bytes 1332000 | tf_op jit(solution)/shard_map/reduce_sum | solution.py:620
  146.1 0.5 broadcast_multiply_fusion
  146.6 4.0 %copy.9 = bf16[514,3328]{1,0:T(8,128)(2,1)} copy(bf16[514,3328]{1,0:T(8,128)(2,1)} %get-tuple-element.12) | data formatting | bytes 6842368
  (1 shorter events, 0.0 us)
Async XLA Ops:
  5.7 138.3 %copy-start.1 = (bf16[100]{0:T(256)(128)(2,1)S(1)}, bf16[100]{0:T(256)(128)(2,1)}, u32[]{:S(2)}) copy-start(bf16[100]{0:T(256)(128)(2,1)} %param.8) | copy-start | bytes 604
  5.7 138.3 %copy-start = (bf16[1664,100]{0,1:T(8,128)(2,1)S(1)}, bf16[1664,100]{0,1:T(8,128)(2,1)}, u32[]{:S(2)}) copy-start(bf16[1664,100]{0,1:T(8,128)(2,1)} %param.7) | copy-start | bytes 998404

commit v2 on v1

v2 whole, which is shorter than its diff:
```python
import functools
import math

import jax
import jax.numpy as jnp
from jax import lax
from jax.experimental import pallas as pl
from jax.experimental.pallas import tpu as pltpu
from jax.sharding import PartitionSpec as P

HEAD_DIM = 128
TILE = 257
SLOTS = 2
HEADS = 13
WIDTH = HEADS * HEAD_DIM
MODEL = 3200
SHARD = 100
PADDED = 112
N_FSDP = 32
N_DP = 8
ROWS_DEV = SLOTS * TILE
WINDOW = 258
STARTS = (0, 256)
COMMON = 640
PARITY = 512
PAIRS = (((0, 512), (512, 384)), ((896, 384), (1280, 384)))
SPLIT = 7
TOP = 64
BOTTOM = PADDED - TOP
PIECE = 16
MIB = 1024 * 1024
F32 = jnp.float32
BF16 = jnp.bfloat16
MESH = pl.DeviceIdType.MESH


def dot(a, b, dims):
    return lax.dot_general(a, b, (dims, ((), ())), preferred_element_type=F32)


def selection(tile, transposed):
    first = 128 * tile
    owner = first // PADDED
    base = owner * SHARD + jnp.minimum(first - owner * PADDED, SHARD - 1)
    source_tile = jnp.minimum(base // 128, MODEL // 128 - 2)
    shape = (128, 256) if transposed else (256, 128)
    line = (128, 1) if transposed else (1, 128)
    target = lax.broadcasted_iota(jnp.int32, line, 0 if transposed else 1) + first
    wanted = jnp.full(line, -1, jnp.int32)
    for step in range(3):
        index = owner + step
        inside = (target >= index * PADDED) & (target < index * PADDED + SHARD)
        place = target - index * (PADDED - SHARD) - source_tile * 128
        wanted = jnp.where(inside, place, wanted)
    source = lax.broadcasted_iota(jnp.int32, shape, 1 if transposed else 0)
    chosen = jnp.where(source == wanted, 1.0, 0.0)
    columns = pl.ds(pl.multiple_of(source_tile * 128, 128), 256)
    return chosen.astype(BF16), columns


def spread_cotangent(cot_ref, padded_ref):
    def one_tile(tile, carry):
        chooser, source = selection(tile, False)
        columns = pl.ds(pl.multiple_of(tile * 128, 128), 128)
        padded_ref[:, columns] = dot(cot_ref[:, source], chooser, ((1,), (0,))).astype(BF16)
        return carry

    lax.fori_loop(0, N_FSDP * PADDED // 128, one_tile, 0)


def with_ones(values):
    return jnp.concatenate([values, jnp.ones_like(values)], axis=1)


def store_window(ref, slot, columns, values, keep):
    start = STARTS[slot]
    if not keep:
        ref[start : start + WINDOW, columns] = values
    elif slot == 0:
        kept = ref[256:WINDOW, columns]
        row = lax.broadcasted_iota(jnp.int32, kept.shape, 0)
        ref[0:256, columns] = values[0:256]
        ref[256:WINDOW, columns] = jnp.where(row == 1, kept, values[256:WINDOW])
    else:
        kept = ref[256:272, columns]
        row = lax.broadcasted_iota(jnp.int32, kept.shape, 0)
        ref[256 : 256 + WINDOW, columns] = values
        ref[256:272, columns] = jnp.where(row == 0, kept, values[0:16])


def head_columns(third, head):
    return pl.ds(pl.multiple_of(third * WIDTH + head * HEAD_DIM, 128), HEAD_DIM)


def forward_heads(qkv_ref, live, attended_ref, probs_ref, first, last):
    factor = math.log2(math.e) / math.sqrt(HEAD_DIM)

    def one_head(head, carry):
        scores, powers, both = [], [], []
        for start in STARTS:
            rows = slice(start, start + WINDOW)
            queries = qkv_ref[rows, head_columns(0, head)]
            keys = qkv_ref[rows, head_columns(1, head)]
            scores.append(dot(queries, keys, ((1,), (1,))))
        for slot in range(SLOTS):
            out_of_tile = WINDOW - 1 if slot == 0 else 0
            column = lax.broadcasted_iota(jnp.int32, (1, WINDOW), 1)
            masked = jnp.where(column == out_of_tile, -1e30, scores[slot])
            top = jnp.max(masked, axis=1, keepdims=True)
            powers.append(jnp.exp2((masked - top) * factor))
        for slot, start in enumerate(STARTS):
            values = qkv_ref[start : start + WINDOW, head_columns(2, head)]
            both.append(dot(powers[slot].astype(BF16), with_ones(values), ((1,), (0,))))
        for slot in range(SLOTS):
            out_of_tile = WINDOW - 1 if slot == 0 else 0
            row = lax.broadcasted_iota(jnp.int32, (WINDOW, HEAD_DIM), 0)
            share = jnp.where(row == out_of_tile, 0.0, 1.0 / both[slot][:, HEAD_DIM:])
            for start in range(0, WINDOW, HEAD_DIM):
                size = min(HEAD_DIM, WINDOW - start)
                probs = powers[slot][:, start : start + size] * share[:, 0:size]
                probs_ref[slot * HEADS + head, :, start : start + size] = probs.astype(BF16)
            attended = jnp.where(live > slot, both[slot][:, :HEAD_DIM] * share, 0.0)
            store_window(
                attended_ref, slot, head_columns(0, head), attended.astype(BF16), slot == 1
            )
        return carry

    lax.fori_loop(first, last, one_head, 0)


def turn_cotangent(cot_ref, turned_ref):
    def one_tile(tile, carry):
        chooser, source = selection(tile, True)
        rows = pl.ds(pl.multiple_of(tile * 128, 128), 128)
        turned_ref[rows, :] = dot(chooser, cot_ref[:, source], ((1,), (1,))).astype(BF16)
        return carry

    lax.fori_loop(0, N_FSDP * PADDED // 128, one_tile, 0)


def weight_partials(turned_ref, attended_ref, partial_ref, lanes, first, last):
    height = N_FSDP * PADDED // 4

    def one_line(line, carry):
        rows = pl.ds(pl.multiple_of(line * height, height), height)
        for start in range(lanes.start, lanes.stop, 256):
            size = min(256, lanes.stop - start)
            columns = slice(start, start + size)
            sums = dot(turned_ref[rows, :], attended_ref[:, columns], ((1,), (0,)))
            partial_ref[line, :, :, :, columns] = sums.astype(BF16).reshape(4, 2, PADDED, size)
        return carry

    lax.fori_loop(first, last, one_line, 0)


def attended_grads(padded_ref, weight_ref, d_attended_ref, first, last):
    def one_block(columns, size):
        right = weight_ref[:, :, :, :, columns].reshape(N_FSDP * PADDED, size)
        d_attended_ref[:, columns] = dot(padded_ref[...], right, ((1,), (0,))).astype(BF16)

    def one_full(index, carry):
        one_block(pl.ds(pl.multiple_of(index * 256, 256), 256), 256)
        return carry

    lax.fori_loop(first, min(last, WIDTH // 256), one_full, 0)
    if last > WIDTH // 256 and WIDTH % 256:
        one_block(slice(WIDTH // 256 * 256, WIDTH), WIDTH % 256)


def backward_heads(qkv_ref, live, probs_ref, attended_ref, grad_ref, first, last):
    inverse = 1.0 / math.sqrt(HEAD_DIM)

    def one_head(head, carry):
        products, grads = [], []
        for start in STARTS:
            rows = slice(start, start + WINDOW)
            values = qkv_ref[rows, head_columns(2, head)]
            d_attended = grad_ref[rows, head_columns(0, head)]
            attended = attended_ref[rows, head_columns(0, head)]
            taken = -(d_attended.astype(F32) * attended.astype(F32))
            left = jnp.concatenate([d_attended, taken.astype(BF16)], axis=1)
            products.append(dot(left, with_ones(values), ((1,), (1,))))
        for slot, start in enumerate(STARTS):
            rows = slice(start, start + WINDOW)
            queries = qkv_ref[rows, head_columns(0, head)]
            keys = qkv_ref[rows, head_columns(1, head)]
            probs = probs_ref[slot * HEADS + head].astype(F32)
            d_scores = (probs * products[slot]).astype(BF16)
            grad_query = dot(d_scores, keys, ((1,), (0,))) * inverse
            grad_key = dot(d_scores, queries, ((0,), (0,))) * inverse
            grads.append(
                [jnp.where(live > slot, grad, 0.0).astype(BF16) for grad in (grad_query, grad_key)]
            )
        for slot in (1, 0):
            for third in (0, 1):
                store_window(grad_ref, slot, head_columns(third, head), grads[slot][third], True)
        return carry

    lax.fori_loop(first, last, one_head, 0)


class Copies:
    def __init__(self, send_sems, recv_sems):
        self.send_sems, self.recv_sems, self.count, self.made = send_sems, recv_sems, 0, []

    def start(self, source, target, device):
        copy = pltpu.make_async_remote_copy(
            src_ref=source,
            dst_ref=target,
            send_sem=self.send_sems.at[self.count],
            recv_sem=self.recv_sems.at[self.count],
            device_id=device,
            device_id_type=MESH,
        )
        copy.start()
        self.count += 1
        self.made.append(copy)
        return copy

    def finish(self):
        for copy in self.made:
            copy.wait_send()


class Place:
    def __init__(self):
        self.f = lax.axis_index("fsdp")
        self.z = lax.axis_index("dp")
        self.c = lax.rem(self.f, 2)
        chip = self.f // 2
        self.y = lax.rem(chip, 4)
        self.x = chip // 4

    def device(self, x, y, c):
        return (self.z, ((x * 4) + y) * 2 + c)

    def around(self, axis, steps):
        u = lax.rem((self.x if axis == 0 else self.y) + 4 + steps, 4)
        return u

    def neighbour(self, axis, steps):
        u = self.around(axis, steps)
        return self.device(u, self.y, self.c) if axis == 0 else self.device(self.x, u, self.c)

    def sibling(self):
        return self.device(self.x, self.y, 1 - self.c)

    def layer(self, steps):
        return lax.rem(self.z + steps, N_DP)

    def greet(self):
        barrier = pltpu.get_barrier_semaphore()
        others = [self.sibling()]
        for axis in (0, 1):
            for step in (1, -1):
                others.append(self.neighbour(axis, step))
        for step in range(1, N_DP):
            others.append((self.layer(step), self.f))
        for other in others:
            pl.semaphore_signal(barrier, inc=1, device_id=other, device_id_type=MESH)
        pl.semaphore_wait(barrier, len(others))


def pick(first, u, v):
    return (u, v) if first == 0 else (v, u)


class WeightGather:
    def __init__(self, place, copies, weight_ref):
        self.place, self.copies, self.weight = place, copies, weight_ref
        self.own = (place.x, place.y)
        self.last, self.shared, self.lifted = {}, [], {}
        parity = lax.rem(place.z, 2)
        self.table = (slice(0, COMMON), self.lanes_of(parity), self.lanes_of(1 - parity))

    def lanes_of(self, parity):
        return pl.ds(pl.multiple_of(COMMON + PARITY * parity, 128), PARITY)

    def block(self, half, x, y, rows=slice(0, PADDED)):
        return self.weight.at[x, y, self.place.c, rows, self.table[half]]

    def send(self, half, axis, step, x, y, rows=slice(0, PADDED)):
        ref = self.block(half, x, y, rows)
        return self.copies.start(ref, ref, self.place.neighbour(axis, step))

    def begin(self):
        self.first = {}
        self.second = {}
        for half in (0, 1):
            for step in (1, -1):
                self.first[half, step] = self.send(half, half, step, *self.own)
        for half in (0, 1):
            self.send_second(half, 0)

    def send_second(self, half, away):
        u, v = self.place.around(half, away), self.place.around(1 - half, 0)
        for step in (1, -1):
            self.second[half, away, step] = self.send(half, 1 - half, step, *pick(half, u, v))

    def middle(self):
        self.far = {}
        place = self.place
        for step in (1, -1):
            for half in (0, 1):
                self.first[half, step].wait_recv()
                u, v = place.around(half, -step), place.around(1 - half, 0)
                part = slice(0, TOP) if step == 1 else slice(TOP, PADDED)
                self.far[half, step] = self.send(half, half, step, *pick(half, u, v), part)
                self.send_second(half, -step)

    def farthest(self):
        for half in (0, 1):
            for step in (1, -1):
                self.far[half, step].wait_recv()
            self.send_second(half, 2)

    def spread(self, away):
        place = self.place
        for half in (0, 1):
            for step in (1, -1):
                self.second[half, away, step].wait_recv()
                u, v = place.around(half, away), place.around(1 - half, -step)
                part = slice(0, TOP) if step == 1 else slice(TOP, PADDED)
                self.last[half, away, step] = self.send(
                    half, 1 - half, step, *pick(half, u, v), part
                )

    def share(self, away):
        place = self.place
        for half in (1, 0):
            for step in (1, -1):
                self.last[half, away, step].wait_recv()
            u = place.around(half, away)
            if half == 1:
                self.lifted[away] = []
                for step, part in ((1, slice(0, 2)), (N_DP - 1, slice(2, 4))):
                    ref = self.weight.at[part, u, place.c, :, self.table[1]]
                    self.lifted[away].append(
                        self.copies.start(ref, ref, (place.layer(step), place.f))
                    )
            line = (u, slice(None)) if half == 0 else (slice(None), u)
            self.give(line, half)

    def give(self, line, half):
        ref = self.weight.at[*line, self.place.c, :, self.table[half]]
        self.shared.append(self.copies.start(ref, ref, self.place.sibling()))

    def cross(self, away):
        for copy in self.lifted[away]:
            copy.wait_recv()
        self.give((slice(None), self.place.around(1, away)), 2)

    def end(self):
        for copy in self.shared:
            copy.wait_recv()


class GradReduce:
    def __init__(
        self, place, copies, table, partial_ref, sums_ref, buffers, layers_ref, result_ref
    ):
        self.place, self.copies, self.table = place, copies, table
        self.whole = slice(table[0][0], table[1][0] + table[1][1])
        self.partial, self.sums, self.buffers = partial_ref, sums_ref, buffers
        self.layers, self.result = layers_ref, result_ref

    def line(self, half, away):
        u = self.place.around(half, away)
        return (u, slice(None)) if half == 0 else (slice(None), u)

    def lanes(self, half):
        return slice(self.table[half][0], self.table[half][0] + self.table[half][1])

    def begin(self):
        self.crossed = {}
        for away in (2, 1, -1, 0):
            for half in (0, 1):
                line, lanes = self.line(half, away), self.lanes(half)
                self.crossed[half, away] = self.copies.start(
                    self.partial.at[*line, 1 - self.place.c, :, lanes],
                    self.sums.at[*line, :, lanes],
                    self.place.sibling(),
                )

    def chunk(self, half, away, v):
        u = self.place.around(half, away)
        return pick(half, u, v)

    def add_own(self, half, away):
        self.crossed[half, away].wait_recv()
        lanes = self.lanes(half)

        def one(v, carry):
            x, y = self.chunk(half, away, v)
            self.sums[x, y, :, lanes] += self.partial[x, y, self.place.c, :, lanes]
            return carry

        lax.fori_loop(0, 4, one, 0)

    def group(self, half, away, first):
        u = self.place.around(half, away)
        part = slice(first, first + 2)
        return self.sums.at[*pick(half, u, part), :, self.lanes(half)]

    def sends_far(self):
        self.near, self.far = {}, {}
        place = self.place
        for half in (0, 1):
            self.add_own(half, 2)
            for step in (1, -1):
                self.far[half, step] = self.copies.start(
                    self.group(half, 2, 0 if step == 1 else 2),
                    self.buffers[half][0].at[0 if step == 1 else 1],
                    place.neighbour(half, step),
                )

    def sends_near(self):
        place = self.place
        for step in (1, -1):
            for half in (0, 1):
                self.add_own(half, step)
                other = 2 if step == 1 else 0
                self.near[half, step, 0] = self.copies.start(
                    self.group(half, step, other),
                    self.buffers[half][1].at[0 if step == 1 else 1, slice(other, other + 2)],
                    place.neighbour(half, step),
                )

    def own_line(self):
        for half in (0, 1):
            self.add_own(half, 0)

    def first_forward(self):
        place = self.place
        for step in (1, -1):
            for half in (0, 1):
                side, start = (0, 0) if step == 1 else (1, 2)
                self.far[half, step].wait_recv()
                lanes = self.lanes(half)
                arrived = self.buffers[half][0]

                def one(v, carry, half=half, side=side, start=start, lanes=lanes, arrived=arrived):
                    x, y = self.chunk(half, step, start + v)
                    self.sums[x, y, :, lanes] += arrived[side, v]
                    return carry

                lax.fori_loop(0, 2, one, 0)
                self.near[half, step, 1] = self.copies.start(
                    self.group(half, step, start),
                    self.buffers[half][1].at[side, slice(start, start + 2)],
                    place.neighbour(half, step),
                )

    def first_end(self):
        for half in (0, 1):
            for step in (1, -1):
                self.near[half, step, 0].wait_recv()
                self.near[half, step, 1].wait_recv()
            lanes = self.lanes(half)
            arrived = self.buffers[half][1]

            def one(v, carry, half=half, lanes=lanes, arrived=arrived):
                x, y = self.chunk(half, 0, v)
                total = self.sums[x, y, :, lanes].astype(F32)
                total += arrived[0, v].astype(F32) + arrived[1, v].astype(F32)
                self.sums[x, y, :, lanes] = total.astype(BF16)
                return carry

            lax.fori_loop(0, 4, one, 0)
            self.second_sends(half)

    def mine(self, half, away):
        place = self.place
        return pick(half, place.around(half, 0), place.around(1 - half, away))

    def second_sends(self, half):
        place, lanes = self.place, self.lanes(half)
        if half == 0:
            self.far2, self.near2 = {}, {}
        for step in (1, -1):
            side = 0 if step == 1 else 1
            rows = slice(0, TOP) if step == 1 else slice(TOP, PADDED)
            self.far2[half, step] = self.copies.start(
                self.sums.at[*self.mine(half, 2), rows, lanes],
                self.buffers[half][2].at[rows],
                place.neighbour(1 - half, step),
            )
        for step in (1, -1):
            side = 0 if step == 1 else 1
            rows = slice(TOP, PADDED) if step == 1 else slice(0, TOP)
            self.near2[half, step, 0] = self.copies.start(
                self.sums.at[*self.mine(half, step), rows, lanes],
                self.buffers[half][3].at[side, rows],
                place.neighbour(1 - half, step),
            )

    def second_forward(self):
        place = self.place
        for half in (0, 1):
            lanes = self.lanes(half)
            for step in (1, -1):
                side = 0 if step == 1 else 1
                rows = slice(0, TOP) if step == 1 else slice(TOP, PADDED)
                self.far2[half, step].wait_recv()
                x, y = self.mine(half, step)
                self.sums[x, y, rows, lanes] += self.buffers[half][2][rows]
                self.near2[half, step, 1] = self.copies.start(
                    self.sums.at[x, y, rows, lanes],
                    self.buffers[half][3].at[side, rows],
                    place.neighbour(1 - half, step),
                )

    def second_end(self):
        layers = self.layers
        layers[0, PADDED:128, :] = jnp.zeros((128 - PADDED, layers.shape[2]), BF16)
        for half in (0, 1):
            lanes = self.lanes(half)
            for step in (1, -1):
                self.near2[half, step, 0].wait_recv()
                self.near2[half, step, 1].wait_recv()
            x, y = self.mine(half, 0)
            arrived = self.buffers[half][3]
            total = self.sums[x, y, :, lanes].astype(F32)
            total += arrived[0].astype(F32) + arrived[1].astype(F32)
            local = slice(lanes.start - self.whole.start, lanes.stop - self.whole.start)
            layers[0, 0:PADDED, local] = total.astype(BF16)

    def piece(self, z):
        return pl.ds(pl.multiple_of(z * PIECE, PIECE), PIECE)

    def layer_sends(self):
        place = self.place
        self.up = [
            self.copies.start(
                self.layers.at[0, self.piece(place.layer(step))],
                self.layers.at[1, slice(step * PIECE, step * PIECE + PIECE)],
                (place.layer(step), place.f),
            )
            for step in range(1, N_DP)
        ]

    def layer_sums(self):
        place = self.place
        own = self.piece(place.z)
        total = self.layers[0, own, :].astype(F32)
        for step in range(1, N_DP):
            self.up[step - 1].wait_recv()
            total += self.layers[1, step * PIECE : step * PIECE + PIECE, :].astype(F32)
        self.result[own, self.whole] = total.astype(BF16)
        self.down = [
            self.copies.start(
                self.result.at[own, self.whole],
                self.result.at[own, self.whole],
                (place.layer(step), place.f),
            )
            for step in range(1, N_DP)
        ]

    def end(self):
        for copy in self.down:
            copy.wait_recv()


N_COPIES = 48 + 12 + 2 * (8 + 12 + 12 + 14)


def whole_kernel(counts_ref, matrix_ref, gain_ref, qkv_ref, cot_ref, *refs):
    grad_ref, grad_weight_ref, grad_scale_ref = refs[:3]
    weight_ref, partial_ref, sums_ref, result_ref, padded_ref, turned_ref = refs[3:9]
    attended_ref, probs_ref, send_sems, recv_sems, load_sem = refs[9:14]
    buffers = refs[14:]
    held_ref = grad_ref
    load = pltpu.make_async_copy(cot_ref, grad_ref.at[:, 0:MODEL], load_sem)
    load.start()
    place = Place()
    copies = Copies(send_sems, recv_sems)
    gain = gain_ref[:, 0:1]
    shard = (matrix_ref[...].astype(F32) * gain).astype(BF16)
    weight_ref[place.x, place.y, place.c, 0:SHARD] = shard
    weight_ref[place.x, place.y, place.c, SHARD:PADDED] = jnp.zeros(
        (PADDED - SHARD, WIDTH), BF16
    )
    place.greet()
    live = jnp.full((1, HEAD_DIM), counts_ref[place.z * N_FSDP + place.f], jnp.int32)
    gather = WeightGather(place, copies, weight_ref)
    early, late = [
        GradReduce(
            place, copies, PAIRS[i], partial_ref, sums_ref,
            (buffers[9 * i : 9 * i + 4], buffers[9 * i + 4 : 9 * i + 8]), buffers[9 * i + 8],
            result_ref,
        )
        for i in (0, 1)
    ]

    def forward(first, last):
        forward_heads(qkv_ref, live, attended_ref, probs_ref, first, last)

    def backward(first, last):
        backward_heads(qkv_ref, live, probs_ref, attended_ref, grad_ref, first, last)

    def d_attended(first, last):
        attended_grads(padded_ref, weight_ref, grad_ref, first, last)

    def partials(lanes, first, last):
        weight_partials(turned_ref, attended_ref, partial_ref, lanes, first, last)

    gather.begin()
    forward(0, 3)
    gather.middle()
    forward(3, SPLIT)
    gather.farthest()
    load.wait()
    turn_cotangent(held_ref, turned_ref)
    gather.spread(0)
    partials(early.whole, 0, 2)
    gather.spread(-1)
    gather.spread(1)
    partials(early.whole, 2, 4)
    early.begin()
    gather.share(0)
    gather.spread(2)
    forward(SPLIT, 10)
    gather.share(-1)
    gather.share(1)
    early.sends_far()
    forward(10, HEADS)
    early.sends_near()
    gather.share(2)
    partials(late.whole, 0, 2)
    early.own_line()
    early.first_forward()
    gather.cross(0)
    gather.cross(-1)
    partials(late.whole, 2, 4)
    late.begin()
    gather.cross(1)
    spread_cotangent(held_ref, padded_ref)
    late.sends_far()
    early.first_end()
    gather.cross(2)
    late.sends_near()
    late.own_line()
    gather.end()
    d_attended(0, 2)
    late.first_forward()
    early.second_forward()
    d_attended(2, 4)
    early.second_end()
    early.layer_sends()
    late.first_end()
    d_attended(4, 7)
    late.second_forward()
    backward(0, 3)
    early.layer_sums()
    late.second_end()
    late.layer_sends()
    backward(3, 9)
    late.layer_sums()
    backward(9, HEADS)
    early.end()
    late.end()
    summed = result_ref[0:SHARD, :].astype(F32)
    factor = 8.0 / math.sqrt(ROWS_DEV * N_FSDP * N_DP)
    grad_weight_ref[...] = factor * gain * summed
    total = factor * jnp.sum(matrix_ref[...].astype(F32) * summed, axis=1, keepdims=True)
    grad_scale_ref[...] = jnp.broadcast_to(total, (SHARD, 128))
    copies.finish()


def exchange_buffers():
    shapes = []
    for table in PAIRS:
        for _, size in table:
            shapes += [
                pltpu.VMEM((2, 2, PADDED, size), BF16),
                pltpu.VMEM((2, 4, PADDED, size), BF16),
                pltpu.VMEM((PADDED, size), BF16),
                pltpu.VMEM((2, PADDED, size), BF16),
            ]
        shapes.append(pltpu.VMEM((2, 128, table[0][1] + table[1][1]), BF16))
    return shapes


VMEM = pl.BlockSpec(memory_space=pltpu.VMEM)


def whole(counts, matrix, gain, qkv, cot):
    return pl.pallas_call(
        whole_kernel,
        out_shape=(
            jax.ShapeDtypeStruct((ROWS_DEV, 2 * WIDTH), BF16),
            jax.ShapeDtypeStruct((SHARD, WIDTH), F32),
            jax.ShapeDtypeStruct((SHARD, 128), F32),
        ),
        in_specs=[pl.BlockSpec(memory_space=pltpu.SMEM)] + [VMEM] * 3 + [pl.BlockSpec(memory_space=pl.ANY)],
        out_specs=[VMEM] * 3,
        scratch_shapes=[
            pltpu.VMEM((4, 4, 2, PADDED, WIDTH), BF16),
            pltpu.VMEM((4, 4, 2, PADDED, WIDTH), BF16),
            pltpu.VMEM((4, 4, PADDED, WIDTH), BF16),
            pltpu.VMEM((128, WIDTH), BF16),
            pltpu.VMEM((ROWS_DEV, N_FSDP * PADDED), BF16),
            pltpu.VMEM((N_FSDP * PADDED, ROWS_DEV), BF16),
            pltpu.VMEM((ROWS_DEV, WIDTH), BF16),
            pltpu.VMEM((SLOTS * HEADS, WINDOW, WINDOW), BF16),
            pltpu.SemaphoreType.DMA((N_COPIES,)),
            pltpu.SemaphoreType.DMA((N_COPIES,)),
            pltpu.SemaphoreType.DMA,
        ]
        + exchange_buffers(),
        compiler_params=pltpu.CompilerParams(
            collective_id=0, has_side_effects=True, vmem_limit_bytes=62 * MIB
        ),
        name="whole",
    )(counts, matrix, gain, qkv, cot)


def body(query_key_value, cotangent, output_weight, layer_scale, tile_counts):
    gain = jnp.broadcast_to(layer_scale.astype(F32)[:, None], (SHARD, 128))
    grads, grad_weight, grad_scale = whole(
        tile_counts, output_weight.T, gain, query_key_value, cotangent
    )
    return (grads, grad_weight.T, grad_scale[:, 0])


def solution(mesh):
    in_specs = (P(("dp", "fsdp"), None), P(("dp", "fsdp"), None), P(None, "fsdp"), P("fsdp"), P())
    out_specs = (P(("dp", "fsdp"), None), P(None, "fsdp"), P("fsdp"))
    return jax.shard_map(body, mesh=mesh, in_specs=in_specs, out_specs=out_specs, check_vma=False)
```

time: 154 us -> 116 us (0.75); the launches traced: 151 us -> 115 us
  Pallas kernels: 138 us -> 107 us
  other arithmetic: 5.01 us -> 0 us
    pallas_call x1, Pallas kernels: 138 us -> 107 us  [whole(): pl.pallas_call(whole_kernel, out_shape=(jax.ShapeDtypeStruct((ROWS_DEV, 2...]
    reduce_sum x1 -> x0, other arithmetic: 2.06 us -> none  [body(): grad_scale = factor * jnp.sum(output_weight.astype(F32) * summed, axis=0)]
    unnamed x5 -> x4, local copies, waits for them, and re-layouts: 3.98 us -> 4.89 us
where the time goes in v2:
time: 116 us; the launch traced here: 115 us
  Pallas kernels  107 us (92%)
  local copies, waits for them, and re-layouts  7.68 us (7%)
    pallas_call x1, Pallas kernels, whole(): pl.pallas_call(whole_kernel, out_shape=(jax.ShapeDtypeStruct((ROWS_DEV, 2...  107 us
    unnamed x4, local copies, waits for them, and re-layouts  4.89 us

profile of v2, /device:TPU:2, one launch (start us, length us, event | category | flops | bytes accessed | tf_op | source)
XLA Modules:
  0.0 114.9 jit_solution(18042481203380147579)
XLA Ops:
  0.6 1.4 %broadcast_in_dim.2.gain_ref = f32[100,128]{1,0:T(8,128)} broadcast(bf16[100]{0:T(256)(128)(2,1)} %param.8), dimensions={0} | broadcast | bytes 51400 | tf_op jit(solution)/shard_map/broadcast_in_dim | solution.py:719
  2.0 106.6 %whole.1 = (bf16[514,3328]{1,0:T(8,128)(2,1)}, f32[100,1664]{1,0:T(8,128)}, f32[100,128]{1,0:T(8,128)}) custom-call(s32[256]{0:T(256)} %counts_ref.1, bf16[100,1664]{1,0:T(8,128)(2,1)} %bitcast.3, f32[100,128]{1,0:T(8,128)} %broadcast_in_dim.2.gain_ref, bf16[514,4992]{1,0:T(8,128)(2,1)} %qkv_ref.1, bf16[514,3200]{1,0:T(8,128)(2,1)} %cot_ref.1), custom_call_target="tpu_custom_call" | custom-call | tf_op jit(solution)/shard_map/whole/pallas_call | solution.py:688
  108.6 1.4 %slice_reduce_fusion = f32[100]{0:T(128)} fusion(f32[100,128]{1,0:T(8,128)} %get-tuple-element.8), kind=kLoop, calls=%fused_computation | loop fusion | bytes 800 | tf_op jit(solution)/shard_map/slice | solution.py:723
  110.0 0.0 copy-start
  110.0 4.0 %copy.10 = bf16[514,3328]{1,0:T(8,128)(2,1)} copy(bf16[514,3328]{1,0:T(8,128)(2,1)} %get-tuple-element.12) | data formatting | bytes 6842368
  114.1 0.0 copy-done
  114.1 0.8 copy.11
Async XLA Ops:
  110.0 4.0 %copy-start = (f32[100,1664]{1,0:T(8,128)S(1)}, f32[100,1664]{1,0:T(8,128)}, u32[]{:S(2)}) copy-start(f32[100,1664]{1,0:T(8,128)} %get-tuple-element.7) | copy-start | bytes 1996804

commit v3 on v2

--- a/solution.py
+++ b/solution.py
@@ -21,8 +21,9 @@
 ROWS_DEV = SLOTS * TILE
 WINDOW = 258
 STARTS = (0, 256)
-COMMON = 640
-PARITY = 512
+FIRST = 640
+SECOND = 768
+PARITY = 256
 PAIRS = (((0, 512), (512, 384)), ((896, 384), (1280, 384)))
 SPLIT = 7
 TOP = 64
@@ -271,10 +272,15 @@
         self.own = (place.x, place.y)
         self.last, self.shared, self.lifted = {}, [], {}
         parity = lax.rem(place.z, 2)
-        self.table = (slice(0, COMMON), self.lanes_of(parity), self.lanes_of(1 - parity))
-
-    def lanes_of(self, parity):
-        return pl.ds(pl.multiple_of(COMMON + PARITY * parity, 128), PARITY)
+        self.table = (
+            slice(WIDTH - FIRST, WIDTH),
+            self.lanes_of(PARITY * parity, SECOND),
+            self.lanes_of(SECOND * parity, PARITY),
+            self.lanes_of(SECOND * (1 - parity), PARITY),
+        )
+
+    def lanes_of(self, start, size):
+        return pl.ds(pl.multiple_of(start, 128), size)
 
     def block(self, half, x, y, rows=slice(0, PADDED)):
         return self.weight.at[x, y, self.place.c, rows, self.table[half]]
@@ -334,7 +340,7 @@
             if half == 1:
                 self.lifted[away] = []
                 for step, part in ((1, slice(0, 2)), (N_DP - 1, slice(2, 4))):
-                    ref = self.weight.at[part, u, place.c, :, self.table[1]]
+                    ref = self.weight.at[part, u, place.c, :, self.table[2]]
                     self.lifted[away].append(
                         self.copies.start(ref, ref, (place.layer(step), place.f))
                     )
@@ -348,7 +354,7 @@
     def cross(self, away):
         for copy in self.lifted[away]:
             copy.wait_recv()
-        self.give((slice(None), self.place.around(1, away)), 2)
+        self.give((slice(None), self.place.around(1, away)), 3)
 
     def end(self):
         for copy in self.shared:
@@ -630,33 +636,33 @@
     early.own_line()
     early.first_forward()
     gather.cross(0)
-    gather.cross(-1)
     partials(late.whole, 2, 4)
     late.begin()
-    gather.cross(1)
+    gather.cross(-1)
     spread_cotangent(held_ref, padded_ref)
     late.sends_far()
+    gather.cross(1)
+    late.sends_near()
     early.first_end()
     gather.cross(2)
-    late.sends_near()
     late.own_line()
+    early.second_forward()
+    late.first_forward()
     gather.end()
     d_attended(0, 2)
-    late.first_forward()
-    early.second_forward()
-    d_attended(2, 4)
     early.second_end()
     early.layer_sends()
+    d_attended(2, 4)
     late.first_end()
+    early.layer_sums()
     d_attended(4, 7)
     late.second_forward()
     backward(0, 3)
-    early.layer_sums()
     late.second_end()
     late.layer_sends()
-    backward(3, 9)
+    backward(3, 8)
     late.layer_sums()
-    backward(9, HEADS)
+    backward(8, HEADS)
     early.end()
     late.end()
     summed = result_ref[0:SHARD, :].astype(F32)

time: 116 us -> 118 us (1.017)
  Pallas kernels: 107 us -> 110 us
    pallas_call x1, Pallas kernels: 107 us -> 110 us  [whole(): pl.pallas_call(whole_kernel, out_shape=(jax.ShapeDtypeStruct((ROWS_DEV, 2...]
where the time goes in v3:
time: 118 us
  Pallas kernels  110 us (93%)
  local copies, waits for them, and re-layouts  7.68 us (7%)
    pallas_call x1, Pallas kernels, whole(): pl.pallas_call(whole_kernel, out_shape=(jax.ShapeDtypeStruct((ROWS_DEV, 2...  110 us
    unnamed x4, local copies, waits for them, and re-layouts  4.89 us

profile of v3, /device:TPU:2, one launch (start us, length us, event | category | flops | bytes accessed | tf_op | source)
XLA Modules:
  0.0 117.9 jit_solution(4900971009206711281)
XLA Ops:
  0.6 1.4 %broadcast_in_dim.2.gain_ref = f32[100,128]{1,0:T(8,128)} broadcast(bf16[100]{0:T(256)(128)(2,1)} %param.8), dimensions={0} | broadcast | bytes 51400 | tf_op jit(solution)/shard_map/broadcast_in_dim | solution.py:725
  2.0 109.5 %whole.1 = (bf16[514,3328]{1,0:T(8,128)(2,1)}, f32[100,1664]{1,0:T(8,128)}, f32[100,128]{1,0:T(8,128)}) custom-call(s32[256]{0:T(256)} %counts_ref.1, bf16[100,1664]{1,0:T(8,128)(2,1)} %bitcast.3, f32[100,128]{1,0:T(8,128)} %broadcast_in_dim.2.gain_ref, bf16[514,4992]{1,0:T(8,128)(2,1)} %qkv_ref.1, bf16[514,3200]{1,0:T(8,128)(2,1)} %cot_ref.1), custom_call_target="tpu_custom_call" | custom-call | tf_op jit(solution)/shard_map/whole/pallas_call | solution.py:694
  111.5 1.4 %slice_reduce_fusion = f32[100]{0:T(128)} fusion(f32[100,128]{1,0:T(8,128)} %get-tuple-element.8), kind=kLoop, calls=%fused_computation | loop fusion | bytes 800 | tf_op jit(solution)/shard_map/slice | solution.py:729
  113.0 0.0 copy-start
  113.0 4.0 %copy.10 = bf16[514,3328]{1,0:T(8,128)(2,1)} copy(bf16[514,3328]{1,0:T(8,128)(2,1)} %get-tuple-element.12) | data formatting | bytes 6842368
  117.0 0.0 copy-done
  117.0 0.8 copy.11
Async XLA Ops:
  113.0 4.0 %copy-start = (f32[100,1664]{1,0:T(8,128)S(1)}, f32[100,1664]{1,0:T(8,128)}, u32[]{:S(2)}) copy-start(f32[100,1664]{1,0:T(8,128)} %get-tuple-element.7) | copy-start | bytes 1996804

commit v4 on v3

--- a/solution.py
+++ b/solution.py
@@ -636,33 +636,33 @@
     early.own_line()
     early.first_forward()
     gather.cross(0)
+    gather.cross(-1)
     partials(late.whole, 2, 4)
     late.begin()
-    gather.cross(-1)
+    gather.cross(1)
     spread_cotangent(held_ref, padded_ref)
     late.sends_far()
-    gather.cross(1)
-    late.sends_near()
     early.first_end()
     gather.cross(2)
+    late.sends_near()
     late.own_line()
-    early.second_forward()
-    late.first_forward()
     gather.end()
     d_attended(0, 2)
+    late.first_forward()
+    early.second_forward()
+    d_attended(2, 4)
     early.second_end()
     early.layer_sends()
-    d_attended(2, 4)
     late.first_end()
-    early.layer_sums()
     d_attended(4, 7)
     late.second_forward()
     backward(0, 3)
+    early.layer_sums()
     late.second_end()
     late.layer_sends()
-    backward(3, 8)
+    backward(3, 9)
     late.layer_sums()
-    backward(8, HEADS)
+    backward(9, HEADS)
     early.end()
     late.end()
     summed = result_ref[0:SHARD, :].astype(F32)

time: 118 us -> 114 us (0.966)
  Pallas kernels: 110 us -> 105 us
    pallas_call x1, Pallas kernels: 110 us -> 105 us  [whole(): pl.pallas_call(whole_kernel, out_shape=(jax.ShapeDtypeStruct((ROWS_DEV, 2...]
where the time goes in v4:
time: 114 us; the launch traced here: 113 us
  Pallas kernels  105 us (92%)
  local copies, waits for them, and re-layouts  7.68 us (7%)
    pallas_call x1, Pallas kernels, whole(): pl.pallas_call(whole_kernel, out_shape=(jax.ShapeDtypeStruct((ROWS_DEV, 2...  105 us
    unnamed x4, local copies, waits for them, and re-layouts  4.89 us

profile of v4, /device:TPU:2, one launch (start us, length us, event | category | flops | bytes accessed | tf_op | source)
XLA Modules:
  0.0 113.3 jit_solution(14145635938584051873)
XLA Ops:
  0.6 1.4 %broadcast_in_dim.2.gain_ref = f32[100,128]{1,0:T(8,128)} broadcast(bf16[100]{0:T(256)(128)(2,1)} %param.8), dimensions={0} | broadcast | bytes 51400 | tf_op jit(solution)/shard_map/broadcast_in_dim | solution.py:725
  2.0 104.9 %whole.1 = (bf16[514,3328]{1,0:T(8,128)(2,1)}, f32[100,1664]{1,0:T(8,128)}, f32[100,128]{1,0:T(8,128)}) custom-call(s32[256]{0:T(256)} %counts_ref.1, bf16[100,1664]{1,0:T(8,128)(2,1)} %bitcast.3, f32[100,128]{1,0:T(8,128)} %broadcast_in_dim.2.gain_ref, bf16[514,4992]{1,0:T(8,128)(2,1)} %qkv_ref.1, bf16[514,3200]{1,0:T(8,128)(2,1)} %cot_ref.1), custom_call_target="tpu_custom_call" | custom-call | tf_op jit(solution)/shard_map/whole/pallas_call | solution.py:694
  106.9 1.4 %slice_reduce_fusion = f32[100]{0:T(128)} fusion(f32[100,128]{1,0:T(8,128)} %get-tuple-element.8), kind=kLoop, calls=%fused_computation | loop fusion | bytes 800 | tf_op jit(solution)/shard_map/slice | solution.py:729
  108.4 0.0 copy-start
  108.4 4.0 %copy.10 = bf16[514,3328]{1,0:T(8,128)(2,1)} copy(bf16[514,3328]{1,0:T(8,128)(2,1)} %get-tuple-element.12) | data formatting | bytes 6842368
  112.4 0.0 copy-done
  112.4 0.8 copy.11
Async XLA Ops:
  108.4 4.0 %copy-start = (f32[100,1664]{1,0:T(8,128)S(1)}, f32[100,1664]{1,0:T(8,128)}, u32[]{:S(2)}) copy-start(f32[100,1664]{1,0:T(8,128)} %get-tuple-element.7) | copy-start | bytes 1996804
